TPU v7x, 32 devices: a whole 2x2x4 slice. The times are simulated.
32 devices in a mesh: seq: 8 (over y, x, core), head: 4 (over z).
Axes of the slice: x: 2, y: 2, z: 4, core: 2. Of those that a mesh axis runs over, the one named last changes fastest.
Arguments:
- inputs: bfloat16 [16384, 2048], P('seq'), may hold values from -6 to 6
- w_qkv: bfloat16 [3, 2048, 2048], P(None, None, 'head'), may hold values from -0.125 to 0.125
- norm_gain: float32 [2048], P('head'), may hold values from 0.1 to 1.9
- w_out: bfloat16 [2048, 2048], P('head'), may hold values from -0.125 to 0.125
Outputs:
- mixed: bfloat16 [16384, 2048], P(('seq', 'head'))
All inputs are finite; a program needn't handle non-finite values.
Results may differ from a plain program's by a relative error of at most 0.0067.
Values may be sent and summed in bfloat16 or wider, within the bound.
A program may use at most 128 MiB of HBM per device.

v0:
```python
import jax
import jax.numpy as jnp
from jax import lax
from jax.sharding import PartitionSpec as P

DH = 128
BLK = 256


def carried_in(value, axis, combine, identity):
    length, position = (lax.axis_size(axis), lax.axis_index(axis))
    everything = lax.all_gather(value, axis)
    start = jnp.broadcast_to(jnp.asarray(identity, value.dtype), value.shape)

    def step(k, before):
        reached = k < position
        new = combine(before, everything[k])
        return jnp.where(reached, new, before)

    return lax.fori_loop(0, length, step, start)


def on_device(inputs, w_qkv, norm_gain, w_out):
    hp = lax.Precision.HIGHEST
    tokens_here = inputs.shape[0]
    feats = w_qkv.shape[2]
    heads = feats // DH
    count = tokens_here // BLK
    projected = jnp.einsum("td,pdc->ptc", inputs, w_qkv, preferred_element_type=jnp.float32).astype(
        jnp.bfloat16
    )

    def split(arr):
        return arr.reshape(count, BLK, heads, DH).transpose(0, 2, 1, 3)

    query = split(projected[0])
    keys = split(projected[1])
    values = split(projected[2])
    block_states = jnp.einsum("nhjd,nhje->nhde", keys, values, preferred_element_type=jnp.float32)
    totals = jnp.sum(block_states, axis=0)
    local_prefix = jnp.cumsum(block_states, axis=0) - block_states
    carried = carried_in(totals, "seq", lambda early, later: early + later, jnp.zeros_like(totals))
    before = carried[None] + local_prefix
    lower = jnp.tril(jnp.ones((BLK, BLK), jnp.bool_))
    scores = jnp.einsum("nhid,nhjd->nhij", query, keys, preferred_element_type=jnp.float32)
    scores = jnp.where(lower[None, None], scores, 0.0).astype(jnp.bfloat16)
    intra = jnp.einsum("nhij,nhjd->nhid", scores, values, preferred_element_type=jnp.float32)
    inter = jnp.einsum("nhid,nhde->nhie", query.astype(jnp.float32), before, precision=hp)
    attended = intra + inter
    mean_sq = jnp.mean(attended * attended, axis=-1, keepdims=True)
    gain = norm_gain.reshape(1, heads, 1, DH)
    normed = (attended / jnp.sqrt(mean_sq + 1e-06) * gain).astype(jnp.bfloat16)
    normed = normed.transpose(0, 2, 1, 3).reshape(tokens_here, feats)
    regrouped = lax.all_to_all(normed, "head", split_axis=0, concat_axis=1, tiled=True)
    mixed = jnp.dot(
        regrouped,
        lax.all_gather(w_out, "head", axis=0, tiled=True),
        preferred_element_type=jnp.float32,
    )
    return mixed.astype(jnp.bfloat16)


def solution(mesh):
    return jax.shard_map(
        on_device,
        mesh=mesh,
        in_specs=(P("seq", None), P(None, None, "head"), P("head"), P("head", None)),
        out_specs=P(("seq", "head"), None),
        check_vma=False,
    )
```

profile of v0, /device:TPU:0, one launch (start us, length us, event | category | flops | bytes accessed | tf_op | source)
XLA Modules:
  0.0 272.6 jit_solution(3166271667624948249)
XLA Ops:
  6.5 0.0 all-gather.6.cloned.1.call-start
  6.5 17.5 %convert_bitcast_fusion = bf16[3,2048,512]{1,2,0:T(8,128)(2,1)S(1)} fusion(bf16[3,2048,512]{2,1,0:T(8,128)(2,1)} %param.7, bf16[2048,2048]{1,0:T(8,128)(2,1)} %param.6), kind=kOutput, calls=%fused_computation.4 | convolution fusion | flops 12888047616 | bytes 20971520 | tf_op jit(solution)/shard_map/td,pdc->ptc/dot_general | solution.py:29
  24.0 1.9 fusion.25
  25.9 0.7 copy.37
  26.6 0.0 copy-start
  26.6 0.7 copy.38
  27.3 0.0 copy-start.1
  27.3 0.6 copy-done
  27.9 2.1 fusion.26
  30.0 0.0 copy-done.1
  30.0 0.0 all-gather.6.cloned.1.call-update
  30.1 0.2 all-gather.4.cloned.1.call-start
  30.3 0.5 all-gather.4.cloned.1.call-update
  30.8 3.6 %copy.36 = bf16[64,8,8,256]{3,2,1,0:T(8,128)(2,1)} copy(bf16[64,8,8,256]{3,1,2,0:T(8,128)(2,1)} %bitcast.70) | data formatting | bytes 4194304
  34.5 4.6 %copy.20 = bf16[8,256,4,128]{3,1,2,0:T(8,128)(2,1)} copy(bf16[8,256,4,128]{1,0,3,2:T(8,128)(2,1)} %bitcast.68) | data formatting | bytes 4194304 | tf_op jit(solution)/shard_map/reshape;squeeze | solution.py:34
  39.0 4.5 %copy.21 = bf16[8,256,4,128]{3,1,2,0:T(8,128)(2,1)} copy(bf16[8,256,4,128]{1,0,3,2:T(8,128)(2,1)} %bitcast.65) | data formatting | bytes 4194304 | tf_op jit(solution)/shard_map/reshape;squeeze | solution.py:34
  43.6 1.5 fusion.27
  45.1 7.5 %fusion.4 = f32[8,4,256,128]{2,3,1,0:T(8,128)} fusion(pred[256,256]{1,0:T(8,128)(4,1)S(1)} %iota_compare_fusion, bf16[8,256,4,128]{3,1,2,0:T(8,128)(2,1)} %copy.21, bf16[8,256,4,128]{3,1,2,0:T(8,128)(2,1)} %copy.20, bf16[8,256,4,128]{1,0,3,2:T(8,128)(2,1)} %bitcast.67), kind=kOutput, calls=%fused_computation.5 | convolution fusion | flops 1077936128 | bytes 10551296 | tf_op jit(solution)/shard_map/nhij,nhjd->nhid/dot_general | solution.py:47
  52.6 8.2 %all-gather.6.cloned.1.call-done = f32[32,128,128]{2,1,0:T(8,128)} async-done(((f32[4,128,128]{2,1,0:T(8,128)}), f32[32,128,128]{2,1,0:T(8,128)}) %all-gather.6.cloned.1.call-update) | async-done | bytes 2097168 | tf_op jit(solution)/shard_map/all_gather | solution.py:12
  60.8 8.5 %while.14 = (s32[]{:T(128)}, f32[4,128,128]{2,1,0:T(8,128)S(1)}, s32[]{:T(128)}, f32[8,4,128,128]{3,2,1,0:T(8,128)}, s32[]{:T(128)}, /*index=5*/s32[]{:T(128)}) while((s32[]{:T(128)}, f32[4,128,128]{2,1,0:T(8,128)S(1)}, s32[]{:T(128)}, f32[8,4,128,128]{3,2,1,0:T(8,128)}, s32[]{:T(128)}, /*index=5*/s32[]{:T(128)}) %tuple.43), condition=%wide.region_2.3_spmd.clone, body=%wide.region_1.0_spmd.clone.sunk | while | flops 196612 | bytes 786525 | solution.py:20
  60.8 1.0 add_select_fusion.2
  61.9 1.0 add_select_fusion.2
  62.9 1.0 add_select_fusion.2
  64.0 1.0 add_select_fusion.2
  65.1 1.0 add_select_fusion.2
  66.1 1.0 add_select_fusion.2
  67.2 1.0 add_select_fusion.2
  68.3 1.1 add_select_fusion.2
  69.3 0.0 copy-start.2
  69.4 6.9 %multiply_reduce_fusion = (f32[8,4,256]{2,1,0:T(4,128)S(1)}, f32[8,4,256,128]{2,3,1,0:T(8,128)S(1)}) fusion(f32[8,4,256,128]{2,3,1,0:T(8,128)} %fusion.4, f32[8,4,128,128]{3,2,1,0:T(8,128)} %fusion.27, f32[8,4,128,128]{3,2,1,0:T(8,128)S(1)} %get-tuple-element.112, f32[4,128,128]{2,1,0:T(8,128)S(1)} %get-tuple-element.84, bf16[8,256,4,128]{3,1,2,0:T(8,128)(2,1)} %copy.20), kind=kOutput, calls=%fused_computation.9 | convolution fusion | flops 1614798848 | bytes 14974976 | tf_op jit(solution)/shard_map/nhid,nhde->nhie/dot_general | solution.py:48
  76.3 0.0 copy-done.2
  76.3 0.6 fusion.6
  76.9 2.5 copy.26
  79.4 2.7 %all_to_all.14 = bf16[4,512,512]{2,1,0:T(8,128)(2,1)S(1)} reshape(bf16[8,256,4,128]{3,2,1,0:T(4,128)(2,1)} %copy.26) | data formatting | bytes 4194304 | tf_op jit(solution)/shard_map/all_to_all | solution.py:54
  82.1 107.0 %all_to_all.19 = bf16[4,512,512]{2,1,0:T(8,128)(2,1)} all-to-all(bf16[4,512,512]{2,1,0:T(8,128)(2,1)S(1)} %all_to_all.14), channel_id=1, replica_groups=mesh['seq'=8,'head'=4] {'head'}, dimensions={0} | all-to-all | bytes 4194304 | tf_op jit(solution)/shard_map/all_to_all | solution.py:54
  189.1 2.8 %copy.27 = bf16[512,4,512]{0,2,1:T(8,128)(2,1)S(1)} copy(bf16[512,4,512]{2,0,1:T(8,128)(2,1)} %bitcast.69) | data formatting | bytes 4194304 | tf_op jit(solution)/shard_map/all_to_all | solution.py:54
  191.9 64.7 %all-gather.4.cloned.1.call-done = bf16[2048,2048]{1,0:T(8,128)(2,1)} async-done(((bf16[512,2048]{1,0:T(8,128)(2,1)}), bf16[2048,2048]{1,0:T(8,128)(2,1)}) %all-gather.4.cloned.1.call-update) | async-done | bytes 8388624 | tf_op jit(solution)/shard_map/all_gather | solution.py:57
  256.6 9.1 %convolution_convert_fusion = bf16[512,2048]{1,0:T(8,128)(2,1)} fusion(bf16[512,2048]{0,1:T(8,128)(2,1)S(1)} %bitcast.73, bf16[2048,2048]{1,0:T(8,128)(2,1)} %all-gather.4.cloned.1.call-done), kind=kOutput, calls=%fused_computation.13 | convolution fusion | flops 4296015872 | bytes 12582912 | tf_op jit(solution)/shard_map/dot_general | solution.py:55
  (3 shorter events, 0.1 us)
Async XLA Ops:
  6.5 54.3 %all-gather.6.cloned.1.call-start = ((), (), s32[]{:S(2)}) async-start(), calls=%async_computation.2 | async-start | bytes 2359296 | tf_op jit(solution)/shard_map/all_gather | solution.py:12
  26.6 1.3 copy-start
  27.3 2.8 %copy-start.1 = (bf16[64,8,8,256]{3,2,1,0:T(8,128)(2,1)}, bf16[64,8,8,256]{3,2,1,0:T(8,128)(2,1)S(1)}, u32[]{:S(2)}) copy-start(bf16[64,8,8,256]{3,2,1,0:T(8,128)(2,1)S(1)} %copy.38) | copy-start | bytes 6291460
  30.1 226.6 %all-gather.4.cloned.1.call-start = ((), (), s32[]{:S(2)}) async-start(), calls=%async_computation.1 | async-start | bytes 10485760 | tf_op jit(solution)/shard_map/all_gather | solution.py:57
  69.3 6.9 %copy-start.2 = (f32[512]{0:T(512)S(1)}, f32[512]{0:T(512)}, u32[]{:S(2)}) copy-start(f32[512]{0:T(512)} %param.8) | copy-start | bytes 6148
Sparse Core Ops, SparseCore 0:
  30.2 30.5 all-gather.5
  62.4 194.2 all-gather.3
where the time goes:
time: 273 us
  blocking collectives  107 us (39%)
  waiting for transfers between devices  73.4 us (27%)
  matrix products  43.1 us (16%)
  local copies, waits for them, and re-layouts  24.6 us (9%)
  between operations  13.5 us (5%)
  other arithmetic  10.5 us (4%)
    all_to_all x1, blocking collectives, on_device(): lax.all_to_all(normed, 'head', split_axis=0, concat_axis=1, tiled=True)  107 us
    all_gather x1, waiting for transfers between devices, on_device(): lax.all_gather(w_out, 'head', axis=0, tiled=True)  64.7 us
    dot_general x1, matrix products, on_device(): jnp.einsum('td,pdc->ptc', inputs, w_qkv, preferred_element_type=jnp.float32)  17.5 us
    another operation x2, local copies, waits for them, and re-layouts, split(): return arr.reshape(count, BLK, heads, DH).transpose(0, 2, 1, 3)  9.1 us
    dot_general x1, matrix products, on_device(): jnp.dot(regrouped, lax.all_gather(w_out, 'head', axis=0, tiled=True), pre...  9.1 us
    select_n x8, other arithmetic, step(): return jnp.where(reached, new, before)  8.35 us
    all_gather x1, waiting for transfers between devices, carried_in(): everything = lax.all_gather(value, axis)  8.17 us
    dot_general x1, matrix products, on_device(): jnp.einsum('nhij,nhjd->nhid', scores, values, preferred_element_type=jnp....  7.53 us
  transfers between devices with their start and end apart: 2, of which 2 were waited for; matrix products, arithmetic and copies ran while one was open for 16% of the time, Pallas kernels for 0%

commit v1 on v0

--- a/solution.py
+++ b/solution.py
@@ -7,17 +7,11 @@
 BLK = 256
 
 
-def carried_in(value, axis, combine, identity):
+def carried_in(value, axis):
     length, position = (lax.axis_size(axis), lax.axis_index(axis))
     everything = lax.all_gather(value, axis)
-    start = jnp.broadcast_to(jnp.asarray(identity, value.dtype), value.shape)
-
-    def step(k, before):
-        reached = k < position
-        new = combine(before, everything[k])
-        return jnp.where(reached, new, before)
-
-    return lax.fori_loop(0, length, step, start)
+    earlier = (jnp.arange(length) < position).reshape((length,) + (1,) * value.ndim)
+    return jnp.sum(jnp.where(earlier, everything, 0.0), axis=0)
 
 
 def on_device(inputs, w_qkv, norm_gain, w_out):
@@ -26,6 +20,10 @@
     feats = w_qkv.shape[2]
     heads = feats // DH
     count = tokens_here // BLK
+    seqs, heads_axis = lax.axis_size("seq"), lax.axis_size("head")
+    share = w_out.shape[0] // seqs
+    mine = lax.dynamic_slice_in_dim(w_out, lax.axis_index("seq") * share, share, axis=0)
+    w_all = lax.all_gather(mine, ("head", "seq"), axis=0, tiled=True)
     projected = jnp.einsum("td,pdc->ptc", inputs, w_qkv, preferred_element_type=jnp.float32).astype(
         jnp.bfloat16
     )
@@ -39,7 +37,7 @@
     block_states = jnp.einsum("nhjd,nhje->nhde", keys, values, preferred_element_type=jnp.float32)
     totals = jnp.sum(block_states, axis=0)
     local_prefix = jnp.cumsum(block_states, axis=0) - block_states
-    carried = carried_in(totals, "seq", lambda early, later: early + later, jnp.zeros_like(totals))
+    carried = carried_in(totals, "seq")
     before = carried[None] + local_prefix
     lower = jnp.tril(jnp.ones((BLK, BLK), jnp.bool_))
     scores = jnp.einsum("nhid,nhjd->nhij", query, keys, preferred_element_type=jnp.float32)
@@ -52,11 +50,7 @@
     normed = (attended / jnp.sqrt(mean_sq + 1e-06) * gain).astype(jnp.bfloat16)
     normed = normed.transpose(0, 2, 1, 3).reshape(tokens_here, feats)
     regrouped = lax.all_to_all(normed, "head", split_axis=0, concat_axis=1, tiled=True)
-    mixed = jnp.dot(
-        regrouped,
-        lax.all_gather(w_out, "head", axis=0, tiled=True),
-        preferred_element_type=jnp.float32,
-    )
+    mixed = jnp.dot(regrouped, w_all, preferred_element_type=jnp.float32)
     return mixed.astype(jnp.bfloat16)
 
 

time: 273 us -> 184 us (0.67)
  waiting for transfers between devices: 73.4 us -> 11.4 us
  blocking collectives: 107 us -> 85.6 us
  other arithmetic: 10.5 us -> 4.22 us
    all_gather x1, waiting for transfers between devices: 64.7 us -> 0.7 us  [on_device(): w_all = lax.all_gather(mine, ('head', 'seq'), axis=0, tiled=True)]
    all_to_all x1, blocking collectives: 107 us -> 85.6 us  [on_device(): lax.all_to_all(normed, 'head', split_axis=0, concat_axis=1, tiled=True)]
    select_n x8 -> x0, other arithmetic: 8.35 us -> none  [step(): return jnp.where(reached, new, before)]
    unnamed x9 -> x17, local copies, waits for them, and re-layouts: 5.61 us -> 4.5 us
  transfers between devices with their start and end apart: 2 -> 2, of which waited for: 2 -> 2; matrix products, arithmetic and copies ran while one was open for 16% -> 19% of each run, Pallas kernels for 0% -> 0%
where the time goes in v1:
time: 184 us; the launch traced here: 183 us
  blocking collectives  85.6 us (47%)
  matrix products  44.1 us (24%)
  local copies, waits for them, and re-layouts  24.2 us (13%)
  between operations  13.5 us (7%)
  waiting for transfers between devices  11.4 us (6%)
  other arithmetic  4.22 us (2%)
    all_to_all x1, blocking collectives, on_device(): lax.all_to_all(normed, 'head', split_axis=0, concat_axis=1, tiled=True)  85.6 us
    dot_general x1, matrix products, on_device(): jnp.einsum('td,pdc->ptc', inputs, w_qkv, preferred_element_type=jnp.float32)  17.6 us
    all_gather x1, waiting for transfers between devices, carried_in(): everything = lax.all_gather(value, axis)  10.7 us
    dot_general x1, matrix products, on_device(): mixed = jnp.dot(regrouped, w_all, preferred_element_type=jnp.float32)  10 us
    another operation x2, local copies, waits for them, and re-layouts, split(): return arr.reshape(count, BLK, heads, DH).transpose(0, 2, 1, 3)  7.65 us
    dot_general x1, matrix products, on_device(): jnp.einsum('nhij,nhjd->nhid', scores, values, preferred_element_type=jnp....  7.53 us
    all_to_all x2, local copies, waits for them, and re-layouts, on_device(): lax.all_to_all(normed, 'head', split_axis=0, concat_axis=1, tiled=True)  6.94 us
    dot_general x1, matrix products, on_device(): jnp.einsum('nhid,nhde->nhie', query.astype(jnp.float32), before, precisio...  5.51 us
  transfers between devices with their start and end apart: 2, of which 2 were waited for; matrix products, arithmetic and copies ran while one was open for 19% of the time, Pallas kernels for 0%

profile of v1, /device:TPU:0, one launch (start us, length us, event | category | flops | bytes accessed | tf_op | source)
XLA Modules:
  0.0 183.3 jit_solution(1692243192924411163)
XLA Ops:
  6.5 0.0 copy-start
  6.5 0.0 all-gather.6.cloned.1.call-start
  6.5 17.6 %convert_bitcast_fusion = bf16[3,2048,512]{1,2,0:T(8,128)(2,1)S(1)} fusion(bf16[3,2048,512]{2,1,0:T(8,128)(2,1)} %param.5, bf16[2048,2048]{1,0:T(8,128)(2,1)} %param.4), kind=kOutput, calls=%fused_computation.3 | convolution fusion | flops 12888047616 | bytes 20971520 | tf_op jit(solution)/shard_map/td,pdc->ptc/dot_general | solution.py:27
  24.1 1.9 %fusion.25 = (bf16[1,2048,512]{1,2,0:T(8,128)(2,1)S(1)}, bf16[1,2048,512]{1,2,0:T(8,128)(2,1)S(1)}, bf16[1,2048,512]{1,2,0:T(8,128)(2,1)}) fusion(bf16[3,2048,512]{1,2,0:T(8,128)(2,1)S(1)} %convert_bitcast_fusion), kind=kLoop, calls=%fused_computation.31 | loop fusion | bytes 12582912 | tf_op jit(solution)/shard_map/slice | solution.py:36
  26.0 0.7 copy.37
  26.7 0.0 copy-start.3
  26.7 0.7 copy.38
  27.4 0.0 copy-start.4
  27.4 0.6 copy-done.3
  28.1 3.5 %fusion.26 = (f32[4,128,128]{2,1,0:T(8,128)}, f32[8,4,128,128]{3,2,1,0:T(8,128)}) fusion(bf16[8,4,256,128]{2,0,3,1:T(8,128)(2,1)S(1)} %bitcast.62, bf16[8,4,256,128]{2,0,3,1:T(8,128)(2,1)S(1)} %bitcast.60), kind=kOutput, calls=%fused_computation.32 | convolution fusion | flops 268894208 | bytes 6553600 | tf_op jit(solution)/shard_map/nhjd,nhje->nhde/dot_general | solution.py:37
  31.5 0.0 copy-done.4
  31.5 0.0 all-gather.6.cloned.1.call-update
  31.6 0.2 all-gather.4.cloned.1.call-start
  31.8 0.0 copy-done
  31.8 0.7 constant_dynamic-slice_fusion
  32.5 0.0 all-gather.4.cloned.1.call-update
  32.5 2.3 %copy.36 = bf16[64,8,8,256]{3,2,1,0:T(8,128)(2,1)S(1)} copy(bf16[64,8,8,256]{3,1,2,0:T(8,128)(2,1)} %bitcast.66) | data formatting | bytes 4194304
  34.8 3.0 %copy.20 = bf16[8,256,4,128]{3,1,2,0:T(8,128)(2,1)} copy(bf16[8,256,4,128]{1,0,3,2:T(8,128)(2,1)S(1)} %bitcast.64) | data formatting | bytes 4194304 | tf_op jit(solution)/shard_map/reshape;squeeze | solution.py:32
  37.8 0.0 copy-start.2
  37.8 4.7 %copy.21 = bf16[8,256,4,128]{3,1,2,0:T(8,128)(2,1)} copy(bf16[8,256,4,128]{1,0,3,2:T(8,128)(2,1)} %bitcast.61) | data formatting | bytes 4194304 | tf_op jit(solution)/shard_map/reshape;squeeze | solution.py:32
  42.5 0.0 copy-done.2
  42.5 1.5 fusion.27
  44.1 7.5 %fusion.4 = f32[8,4,256,128]{2,3,1,0:T(8,128)} fusion(pred[256,256]{1,0:T(8,128)(4,1)S(1)} %iota_compare_fusion, bf16[8,256,4,128]{3,1,2,0:T(8,128)(2,1)} %copy.21, bf16[8,256,4,128]{3,1,2,0:T(8,128)(2,1)} %copy.20, bf16[8,256,4,128]{1,0,3,2:T(8,128)(2,1)} %bitcast.63), kind=kOutput, calls=%fused_computation.4 | convolution fusion | flops 1077936128 | bytes 10551296 | tf_op jit(solution)/shard_map/nhij,nhjd->nhid/dot_general | solution.py:45
  51.6 10.7 %all-gather.6.cloned.1.call-done = f32[32,128,128]{2,1,0:T(8,128)} async-done(((f32[4,128,128]{2,1,0:T(8,128)}), f32[32,128,128]{2,1,0:T(8,128)}) %all-gather.6.cloned.1.call-update) | async-done | bytes 2097168 | tf_op jit(solution)/shard_map/all_gather | solution.py:12
  62.3 0.0 copy-start.5
  62.3 2.0 %select_reduce_fusion = f32[4,128,128]{2,1,0:T(8,128)S(1)} fusion(f32[8,4,128,128]{3,2,1,0:T(8,128)} %bitcast.69, pred[8]{0:T(512)(128)(4,1)S(1)} %iota_compare_fusion.1), kind=kLoop, calls=%fused_computation.24 | loop fusion | flops 983040 | bytes 2359304 | tf_op jit(solution)/shard_map/reduce_sum | solution.py:14
  64.3 0.2 copy-done.5
  64.5 0.0 copy-start.6
  64.5 5.5 %multiply_reduce_fusion = (f32[8,4,256]{2,1,0:T(4,128)S(1)}, f32[8,4,256,128]{2,3,1,0:T(8,128)S(1)}) fusion(f32[8,4,256,128]{2,3,1,0:T(8,128)} %fusion.4, f32[8,4,128,128]{3,2,1,0:T(8,128)} %fusion.27, f32[8,4,128,128]{3,2,1,0:T(8,128)S(1)} %copy-done.2, f32[4,128,128]{2,1,0:T(8,128)S(1)} %select_reduce_fusion, bf16[8,256,4,128]{3,1,2,0:T(8,128)(2,1)S(1)} %copy-done.5), kind=kOutput, calls=%fused_computation.8 | convolution fusion | flops 1614798848 | bytes 14974976 | tf_op jit(solution)/shard_map/nhid,nhde->nhie/dot_general | solution.py:46
  70.1 0.0 copy-done.6
  70.1 0.6 fusion.6
  70.7 2.5 %copy.26 = bf16[8,256,4,128]{3,2,1,0:T(4,128)(2,1)} copy(bf16[8,256,4,128]{1,3,2,0:T(8,128)(2,1)S(1)} %fusion.6) | data formatting | bytes 4194304 | tf_op jit(solution)/shard_map/convert_element_type | solution.py:50
  73.2 2.8 %all_to_all.14 = bf16[4,512,512]{2,1,0:T(8,128)(2,1)S(1)} reshape(bf16[8,256,4,128]{3,2,1,0:T(4,128)(2,1)} %copy.26) | data formatting | bytes 4194304 | tf_op jit(solution)/shard_map/all_to_all | solution.py:52
  75.9 85.6 %all_to_all.19 = bf16[4,512,512]{2,1,0:T(8,128)(2,1)} all-to-all(bf16[4,512,512]{2,1,0:T(8,128)(2,1)S(1)} %all_to_all.14), channel_id=1, replica_groups=mesh['seq'=8,'head'=4] {'head'}, dimensions={0} | all-to-all | bytes 4194304 | tf_op jit(solution)/shard_map/all_to_all | solution.py:52
  161.5 4.2 %copy.27 = bf16[512,4,512]{0,2,1:T(8,128)(2,1)} copy(bf16[512,4,512]{2,0,1:T(8,128)(2,1)} %bitcast.65) | data formatting | bytes 4194304 | tf_op jit(solution)/shard_map/all_to_all | solution.py:52
  165.7 0.7 all-gather.4.cloned.1.call-done
  166.4 0.0 copy-start.1
  166.4 10.0 %convolution_convert_fusion = bf16[512,2048]{1,0:T(8,128)(2,1)} fusion(bf16[512,2048]{0,1:T(8,128)(2,1)} %bitcast.70, bf16[2048,2048]{1,0:T(8,128)(2,1)} %all-gather.4.cloned.1.call-done), kind=kOutput, calls=%fused_computation.12 | convolution fusion | flops 4296015872 | bytes 12582912 | tf_op jit(solution)/shard_map/dot_general | solution.py:53
  176.4 0.0 copy-done.1
  (3 shorter events, 0.1 us)
Async XLA Ops:
  6.5 25.3 %copy-start = (bf16[512,2048]{1,0:T(8,128)(2,1)S(1)}, bf16[512,2048]{1,0:T(8,128)(2,1)}, u32[]{:S(2)}) copy-start(bf16[512,2048]{1,0:T(8,128)(2,1)} %param.7) | copy-start | bytes 6291460
  6.5 55.8 %all-gather.6.cloned.1.call-start = ((), (), s32[]{:S(2)}) async-start(), calls=%async_computation.2 | async-start | bytes 2359296 | tf_op jit(solution)/shard_map/all_gather | solution.py:12
  26.7 1.4 copy-start.3
  27.4 4.1 %copy-start.4 = (bf16[64,8,8,256]{3,2,1,0:T(8,128)(2,1)}, bf16[64,8,8,256]{3,2,1,0:T(8,128)(2,1)S(1)}, u32[]{:S(2)}) copy-start(bf16[64,8,8,256]{3,2,1,0:T(8,128)(2,1)S(1)} %copy.38) | copy-start | bytes 6291460
  31.6 134.8 %all-gather.4.cloned.1.call-start = ((), (), s32[]{:S(2)}) async-start(), calls=%async_computation.1 | async-start | bytes 8650752 | tf_op jit(solution)/shard_map/all_gather | solution.py:26
  37.8 4.7 %copy-start.2 = (f32[8,4,128,128]{3,2,1,0:T(8,128)S(1)}, f32[8,4,128,128]{3,2,1,0:T(8,128)}, u32[]{:S(2)}) copy-start(f32[8,4,128,128]{3,2,1,0:T(8,128)} %get-tuple-element.9) | copy-start | bytes 6291460
  62.3 2.2 %copy-start.5 = (bf16[8,256,4,128]{3,1,2,0:T(8,128)(2,1)S(1)}, bf16[8,256,4,128]{3,1,2,0:T(8,128)(2,1)}, u32[]{:S(2)}) copy-start(bf16[8,256,4,128]{3,1,2,0:T(8,128)(2,1)} %copy.20) | copy-start | bytes 6291460
  64.5 5.5 %copy-start.6 = (f32[512]{0:T(512)S(1)}, f32[512]{0:T(512)}, u32[]{:S(2)}) copy-start(f32[512]{0:T(512)} %param.6) | copy-start | bytes 6148
  166.4 10.0 %copy-start.1 = (bf16[512,2048]{1,0:T(8,128)(2,1)S(1)}, bf16[512,2048]{1,0:T(8,128)(2,1)}, u32[]{:S(2)}) copy-start(bf16[512,2048]{1,0:T(8,128)(2,1)} %param.7) | copy-start | bytes 6291460
Sparse Core Ops, SparseCore 0:
  31.7 30.5 all-gather.5
  65.2 101.1 all-gather.3

commit v2 on v1

v2 whole, which is shorter than its diff:
```python
import functools

import jax
import jax.numpy as jnp
from jax import lax
from jax.experimental import pallas as pl
from jax.experimental.pallas import tpu as pltpu
from jax.sharding import PartitionSpec as P

DH = 128
BLK = 256
EPS = 1e-06
MESH = pl.DeviceIdType.MESH


def flipped(index, mask):
    out, bit = index, 1
    while bit <= mask:
        if mask & bit:
            out = out + bit * (1 - 2 * ((index // bit) % 2))
        bit *= 2
    return out


def destinations(me, count):
    if count & (count - 1):
        return [lax.rem(me + step, count) for step in range(1, count)] + [me]
    half = count // 2
    masks = list(range(half, count)) + list(range(1, half)) + [0]
    return [flipped(me, mask) for mask in masks]


def mix_kernel(
    seqs, groups, x_hbm, w_hbm, gain_ref, out_ref,
    x_ref, w_ref, q_ref, k_ref, v_ref, prefix, total, outgoing, arrived, ready,
    x_sem, w_sem, own_sem, state_send, state_recv, send_sem, recv_sem,
):
    me, z = lax.axis_index("seq"), lax.axis_index("head")
    tokens, feats = q_ref.shape
    heads = feats // DH
    piece = tokens // groups
    blocks = piece // BLK

    def x_copy(c):
        rows = pl.ds(c * piece, piece)
        return pltpu.make_async_copy(x_hbm.at[rows], x_ref.at[rows], x_sem.at[c])

    def w_copy(p):
        return pltpu.make_async_copy(w_hbm.at[p], w_ref.at[p], w_sem.at[p])

    w_copy(1).start()
    x_copy(0).start()
    w_copy(2).start()
    for c in range(1, groups):
        x_copy(c).start()
    w_copy(0).start()

    barrier = pltpu.get_barrier_semaphore()
    for k in range(seqs):
        @pl.when(k != me)
        def _():
            pl.semaphore_signal(barrier, inc=1, device_id=(k, z), device_id_type=MESH)
    for k in range(groups):
        @pl.when(k != z)
        def _():
            pl.semaphore_signal(barrier, inc=1, device_id=(me, k), device_id_type=MESH)

    total[...] = jnp.zeros_like(total)
    w_copy(1).wait()

    for c in range(groups):
        x_copy(c).wait()
        rows = pl.ds(c * piece, piece)
        k_ref[rows, :] = jnp.dot(
            x_ref[rows, :], w_ref[1], preferred_element_type=jnp.float32
        ).astype(jnp.bfloat16)
        if c == 0:
            w_copy(2).wait()
        v_ref[rows, :] = jnp.dot(
            x_ref[rows, :], w_ref[2], preferred_element_type=jnp.float32
        ).astype(jnp.bfloat16)
        for b in range(blocks):
            n = c * blocks + b
            block = pl.ds(n * BLK, BLK)
            for h in range(heads):
                cols = pl.ds(h * DH, DH)
                before = total[h]
                prefix[n, h] = before
                total[h] = before + lax.dot_general(
                    k_ref[block, cols], v_ref[block, cols],
                    (((0,), (0,)), ((), ())), preferred_element_type=jnp.float32,
                )

    outgoing[...] = total[...].astype(jnp.bfloat16)
    pl.semaphore_wait(barrier, seqs + groups - 2)

    def state_copy(source, target):
        return pltpu.make_async_remote_copy(
            src_ref=outgoing, dst_ref=arrived.at[source],
            send_sem=state_send.at[target], recv_sem=state_recv.at[source],
            device_id=(target, z), device_id_type=MESH,
        )

    for k in reversed(range(seqs)):
        @pl.when(k > me)
        def _():
            state_copy(me, k).start()

    w_copy(0).wait()
    for c in range(groups):
        rows = pl.ds(c * piece, piece)
        q_ref[rows, :] = jnp.dot(
            x_ref[rows, :], w_ref[0], preferred_element_type=jnp.float32
        ).astype(jnp.bfloat16)

    total[...] = jnp.zeros_like(total)
    for k in range(seqs):
        @pl.when(k < me)
        def _():
            state_copy(k, me).wait_recv()
            total[...] += arrived[k].astype(jnp.float32)

    lower = lax.broadcasted_iota(jnp.int32, (BLK, BLK), 0) >= lax.broadcasted_iota(
        jnp.int32, (BLK, BLK), 1
    )

    def attend(n, h):
        block, cols = pl.ds(n * BLK, BLK), pl.ds(h * DH, DH)
        q, v = q_ref[block, cols], v_ref[block, cols]
        scores = lax.dot_general(
            q, k_ref[block, cols], (((1,), (1,)), ((), ())), preferred_element_type=jnp.float32
        )
        scores = jnp.where(lower, scores, 0.0).astype(jnp.bfloat16)
        before = total[h] + prefix[n, h]
        high = before.astype(jnp.bfloat16)
        low = (before - high.astype(jnp.float32)).astype(jnp.bfloat16)
        attended = jnp.dot(scores, v, preferred_element_type=jnp.float32) + jnp.dot(
            jnp.concatenate([q, q], axis=1), jnp.concatenate([high, low], axis=0),
            preferred_element_type=jnp.float32,
        )
        mean_sq = jnp.mean(attended * attended, axis=-1, keepdims=True)
        return (attended * lax.rsqrt(mean_sq + EPS) * gain_ref[:, cols]).astype(jnp.bfloat16)

    def ready_copy(source, target):
        return pltpu.make_async_remote_copy(
            src_ref=ready.at[target],
            dst_ref=out_ref.at[:, pl.ds(source * feats, feats)],
            send_sem=send_sem.at[target], recv_sem=recv_sem.at[source],
            device_id=(me, target), device_id_type=MESH,
        )

    order = destinations(z, groups)
    for target in order:
        for b in range(blocks):
            for h in range(heads):
                ready[target, pl.ds(b * BLK, BLK), pl.ds(h * DH, DH)] = attend(
                    target * blocks + b, h
                )
        if target is not order[-1]:
            ready_copy(z, target).start()
    own = pltpu.make_async_copy(
        ready.at[z], out_ref.at[:, pl.ds(pl.multiple_of(z * feats, feats), feats)], own_sem
    )
    own.start()
    own.wait()
    for target in order[:-1]:
        ready_copy(target, target).wait_recv()
    for target in order[:-1]:
        ready_copy(z, target).wait_send()
    for k in range(seqs):
        @pl.when(k > me)
        def _():
            state_copy(me, k).wait_send()


def on_device(inputs, w_qkv, norm_gain, w_out):
    tokens, width = inputs.shape
    feats = w_qkv.shape[2]
    heads = feats // DH
    seqs, groups = lax.axis_size("seq"), lax.axis_size("head")
    share = w_out.shape[0] // seqs
    mine = lax.dynamic_slice_in_dim(w_out, lax.axis_index("seq") * share, share, axis=0)
    w_all = lax.all_gather(mine, ("head", "seq"), axis=0, tiled=True)
    piece = tokens // groups
    regrouped = pl.pallas_call(
        functools.partial(mix_kernel, seqs, groups),
        out_shape=jax.ShapeDtypeStruct((piece, groups * feats), jnp.bfloat16),
        in_specs=[
            pl.BlockSpec(memory_space=pl.ANY),
            pl.BlockSpec(memory_space=pl.ANY),
            pl.BlockSpec(memory_space=pltpu.VMEM),
        ],
        out_specs=pl.BlockSpec(memory_space=pl.ANY),
        scratch_shapes=[
            pltpu.VMEM((tokens, width), jnp.bfloat16),
            pltpu.VMEM(w_qkv.shape, jnp.bfloat16),
            pltpu.VMEM((tokens, feats), jnp.bfloat16),
            pltpu.VMEM((tokens, feats), jnp.bfloat16),
            pltpu.VMEM((tokens, feats), jnp.bfloat16),
            pltpu.VMEM((tokens // BLK, heads, DH, DH), jnp.float32),
            pltpu.VMEM((heads, DH, DH), jnp.float32),
            pltpu.VMEM((heads, DH, DH), jnp.bfloat16),
            pltpu.VMEM((seqs, heads, DH, DH), jnp.bfloat16),
            pltpu.VMEM((groups, piece, feats), jnp.bfloat16),
            pltpu.SemaphoreType.DMA((groups,)),
            pltpu.SemaphoreType.DMA((3,)),
            pltpu.SemaphoreType.DMA,
            pltpu.SemaphoreType.DMA((seqs,)),
            pltpu.SemaphoreType.DMA((seqs,)),
            pltpu.SemaphoreType.DMA((groups,)),
            pltpu.SemaphoreType.DMA((groups,)),
        ],
        compiler_params=pltpu.CompilerParams(
            collective_id=0, has_side_effects=True, vmem_limit_bytes=56 * 2**20
        ),
        cost_estimate=pl.CostEstimate(
            flops=2 * tokens * feats * (3 * width + 4 * BLK),
            bytes_accessed=2 * (tokens * width + 3 * width * feats) + 200 * 10**6,
            transcendentals=0,
        ),
    )(inputs, w_qkv, norm_gain.reshape(1, feats))
    return jnp.dot(regrouped, w_all, preferred_element_type=jnp.float32).astype(jnp.bfloat16)


def solution(mesh):
    return jax.shard_map(
        on_device,
        mesh=mesh,
        in_specs=(P("seq", None), P(None, None, "head"), P("head"), P("head", None)),
        out_specs=P(("seq", "head"), None),
        check_vma=False,
    )
```

time: 184 us -> 138 us (0.75)
  blocking collectives: 85.6 us -> 0 us
  Pallas kernels: 0 us -> 62.5 us
  waiting for transfers between devices: 11.4 us -> 49.9 us
  matrix products: 44.1 us -> 9.83 us
  local copies, waits for them, and re-layouts: 24.2 us -> 2.31 us
  other arithmetic: 4.22 us -> 0 us
    all_to_all x1 -> x0, blocking collectives: 85.6 us -> none  [on_device(): lax.all_to_all(normed, 'head', split_axis=0, concat_axis=1, tiled=True)]
    pallas_call x0 -> x1, Pallas kernels: none -> 62.5 us  [on_device(): pl.pallas_call(functools.partial(mix_kernel, seqs, groups), out_shape=jax...]
    all_gather x1, waiting for transfers between devices: 0.7 us -> 49.8 us  [on_device(): w_all = lax.all_gather(mine, ('head', 'seq'), axis=0, tiled=True)]
    dot_general x5 -> x1, matrix products: 44.1 us -> 9.83 us  [on_device(): jnp.dot(regrouped, w_all, preferred_element_type=jnp.float32)]
    all_gather x1 -> x0, waiting for transfers between devices: 10.7 us -> none  [carried_in(): everything = lax.all_gather(value, axis)]
    another operation x2 -> x0, local copies, waits for them, and re-layouts: 7.65 us -> none  [split(): return arr.reshape(count, BLK, heads, DH).transpose(0, 2, 1, 3)]
    all_to_all x2 -> x0, local copies, waits for them, and re-layouts: 6.94 us -> none  [on_device(): lax.all_to_all(normed, 'head', split_axis=0, concat_axis=1, tiled=True)]
    unnamed x17 -> x2, local copies, waits for them, and re-layouts: 4.5 us -> 1.59 us
  transfers between devices with their start and end apart: 2 -> 1, of which waited for: 2 -> 1; matrix products, arithmetic and copies ran while one was open for 19% -> 0% of each run, Pallas kernels for 0% -> 45%
where the time goes in v2:
time: 138 us
  Pallas kernels  62.5 us (45%)
  waiting for transfers between devices  49.9 us (36%)
  between operations  13.4 us (10%)
  matrix products  9.83 us (7%)
  local copies, waits for them, and re-layouts  2.31 us (2%)
    pallas_call x1, Pallas kernels, on_device(): pl.pallas_call(functools.partial(mix_kernel, seqs, groups), out_shape=jax...  62.5 us
    all_gather x1, waiting for transfers between devices, on_device(): w_all = lax.all_gather(mine, ('head', 'seq'), axis=0, tiled=True)  49.8 us
    dot_general x1, matrix products, on_device(): jnp.dot(regrouped, w_all, preferred_element_type=jnp.float32)  9.83 us
  transfers between devices with their start and end apart: 1, of which 1 were waited for; matrix products, arithmetic and copies ran while one was open for 0% of the time, Pallas kernels for 45%

profile of v2, /device:TPU:0, one launch (start us, length us, event | category | flops | bytes accessed | tf_op | source)
XLA Modules:
  0.0 137.9 jit_solution(16295357816316207862)
XLA Ops:
  6.5 0.0 copy-start
  6.5 0.0 all-gather.2.cloned.1.call-start
  6.5 1.6 %copy-done = bf16[512,2048]{1,0:T(8,128)(2,1)S(1)} copy-done((bf16[512,2048]{1,0:T(8,128)(2,1)S(1)}, bf16[512,2048]{1,0:T(8,128)(2,1)}, u32[]{:S(2)}) %copy-start) | copy-done | bytes 2097176
  8.1 0.7 constant_dynamic-slice_fusion
  8.8 0.0 all-gather.2.cloned.1.call-update
  8.9 62.5 %shard_map.46 = bf16[512,2048]{1,0:T(8,128)(2,1)} custom-call(bf16[2048,2048]{1,0:T(8,128)(2,1)} %x_hbm.1, bf16[3,2048,512]{2,1,0:T(8,128)(2,1)} %w_hbm.1, f32[1,512]{1,0:T(1,128)} %bitcast.3), custom_call_target="tpu_custom_call" | custom-call | flops 15032385536 | bytes 214680064 | tf_op jit(solution)/shard_map/pallas_call | solution.py:185
  71.4 49.8 %all-gather.2.cloned.1.call-done = bf16[2048,2048]{1,0:T(8,128)(2,1)} async-done(((bf16[64,2048]{1,0:T(8,128)(2,1)}), bf16[2048,2048]{1,0:T(8,128)(2,1)}) %all-gather.2.cloned.1.call-update) | async-done | bytes 8388624 | tf_op jit(solution)/shard_map/all_gather | solution.py:183
  121.3 9.8 %convolution_convert_fusion = bf16[512,2048]{1,0:T(8,128)(2,1)} fusion(bf16[512,2048]{1,0:T(8,128)(2,1)} %shard_map.46, bf16[2048,2048]{1,0:T(8,128)(2,1)} %all-gather.2.cloned.1.call-done), kind=kOutput, calls=%fused_computation | convolution fusion | flops 4296015872 | bytes 12582912 | tf_op jit(solution)/shard_map/dot_general | solution.py:222
Async XLA Ops:
  6.5 1.6 %copy-start = (bf16[512,2048]{1,0:T(8,128)(2,1)S(1)}, bf16[512,2048]{1,0:T(8,128)(2,1)}, u32[]{:S(2)}) copy-start(bf16[512,2048]{1,0:T(8,128)(2,1)} %param.7) | copy-start | bytes 6291460
  6.5 114.7 %all-gather.2.cloned.1.call-start = ((), (), s32[]{:S(2)}) async-start(), calls=%async_computation | async-start | bytes 8650752 | tf_op jit(solution)/shard_map/all_gather | solution.py:183
Sparse Core Ops, SparseCore 0:
  10.2 110.9 all-gather.1

commit v3 on v2

--- a/solution.py
+++ b/solution.py
@@ -31,15 +31,47 @@
 
 
 def mix_kernel(
-    seqs, groups, x_hbm, w_hbm, gain_ref, out_ref,
+    seqs, groups, x_hbm, w_hbm, gain_ref, wo_hbm, out_hbm,
     x_ref, w_ref, q_ref, k_ref, v_ref, prefix, total, outgoing, arrived, ready,
+    landed, wo_ref, acc, out_ref,
     x_sem, w_sem, own_sem, state_send, state_recv, send_sem, recv_sem,
+    along_send, plane_send, pair_send, wo_recv, out_sem,
 ):
     me, z = lax.axis_index("seq"), lax.axis_index("head")
     tokens, feats = q_ref.shape
     heads = feats // DH
     piece = tokens // groups
     blocks = piece // BLK
+    share = feats // seqs
+    chips, chip, core = seqs // 2, me // 2, me % 2
+    order = destinations(z, groups)
+    others = destinations(chip, chips)[:-1]
+
+    def wo_rows(group, seq):
+        return pl.ds(pl.multiple_of(group * feats + seq * share, share), share)
+
+    def own_share():
+        return wo_hbm.at[pl.ds(pl.multiple_of(me * share, share), share)]
+
+    def along_copy(source, target):
+        return pltpu.make_async_remote_copy(
+            src_ref=own_share(), dst_ref=wo_ref.at[wo_rows(source, me)],
+            send_sem=along_send.at[target], recv_sem=wo_recv.at[source, me],
+            device_id=(me, target), device_id_type=MESH,
+        )
+
+    def relay_copy(group, seq, target, send):
+        return pltpu.make_async_remote_copy(
+            src_ref=wo_ref.at[wo_rows(group, seq)], dst_ref=wo_ref.at[wo_rows(group, seq)],
+            send_sem=send, recv_sem=wo_recv.at[group, seq],
+            device_id=(target, z), device_id_type=MESH,
+        )
+
+    def plane_copy(group, other):
+        return relay_copy(group, me, other * 2 + core, plane_send.at[group, other])
+
+    def pair_copy(group, other):
+        return relay_copy(group, other * 2 + core, chip * 2 + 1 - core, pair_send.at[group, other])
 
     def x_copy(c):
         rows = pl.ds(c * piece, piece)
@@ -54,6 +86,8 @@
     for c in range(1, groups):
         x_copy(c).start()
     w_copy(0).start()
+    own_wo = pltpu.make_async_copy(own_share(), wo_ref.at[wo_rows(z, me)], wo_recv.at[z, me])
+    own_wo.start()
 
     barrier = pltpu.get_barrier_semaphore()
     for k in range(seqs):
@@ -66,6 +100,13 @@
             pl.semaphore_signal(barrier, inc=1, device_id=(me, k), device_id_type=MESH)
 
     total[...] = jnp.zeros_like(total)
+    pl.semaphore_wait(barrier, seqs + groups - 2)
+    for target in order[:-1]:
+        along_copy(z, target).start()
+    own_wo.wait()
+    for other in others:
+        plane_copy(z, other).start()
+    pair_copy(z, chip).start()
     w_copy(1).wait()
 
     for c in range(groups):
@@ -92,7 +133,6 @@
                 )
 
     outgoing[...] = total[...].astype(jnp.bfloat16)
-    pl.semaphore_wait(barrier, seqs + groups - 2)
 
     def state_copy(source, target):
         return pltpu.make_async_remote_copy(
@@ -119,6 +159,12 @@
         def _():
             state_copy(k, me).wait_recv()
             total[...] += arrived[k].astype(jnp.float32)
+
+    for group in order[:-1]:
+        along_copy(group, group).wait_recv()
+        for other in others:
+            plane_copy(group, other).start()
+        pair_copy(group, chip).start()
 
     lower = lax.broadcasted_iota(jnp.int32, (BLK, BLK), 0) >= lax.broadcasted_iota(
         jnp.int32, (BLK, BLK), 1
@@ -144,12 +190,11 @@
     def ready_copy(source, target):
         return pltpu.make_async_remote_copy(
             src_ref=ready.at[target],
-            dst_ref=out_ref.at[:, pl.ds(source * feats, feats)],
+            dst_ref=landed.at[source],
             send_sem=send_sem.at[target], recv_sem=recv_sem.at[source],
             device_id=(me, target), device_id_type=MESH,
         )
 
-    order = destinations(z, groups)
     for target in order:
         for b in range(blocks):
             for h in range(heads):
@@ -158,15 +203,48 @@
                 )
         if target is not order[-1]:
             ready_copy(z, target).start()
-    own = pltpu.make_async_copy(
-        ready.at[z], out_ref.at[:, pl.ds(pl.multiple_of(z * feats, feats), feats)], own_sem
-    )
-    own.start()
-    own.wait()
-    for target in order[:-1]:
-        ready_copy(target, target).wait_recv()
+
+    relayed = [z] + order[:-1]
+    for group in relayed:
+        for other in others:
+            relay_copy(group, other * 2 + core, me, plane_send.at[group, other]).wait_recv()
+            pair_copy(group, other).start()
+
+    columns = feats
+    width = out_ref.shape[1]
+    for step, group in enumerate(relayed):
+        for other in others + [chip]:
+            relay_copy(
+                group, other * 2 + 1 - core, me, pair_send.at[group, other]
+            ).wait_recv()
+        if step > 0:
+            ready_copy(group, group).wait_recv()
+        source = ready if step == 0 else landed
+        rows = pl.ds(pl.multiple_of(group * feats, feats), feats)
+        for c in range(width // columns):
+            cols = pl.ds(c * columns, columns)
+            part = jnp.dot(source[group], wo_ref[rows, cols], preferred_element_type=jnp.float32)
+            if step > 0:
+                part += acc[:, cols]
+            if step < groups - 1:
+                acc[:, cols] = part
+            else:
+                out_ref[:, cols] = part.astype(jnp.bfloat16)
+                pltpu.make_async_copy(
+                    out_ref.at[:, cols], out_hbm.at[:, cols], out_sem.at[c]
+                ).start()
+    for c in range(width // columns):
+        cols = pl.ds(c * columns, columns)
+        pltpu.make_async_copy(out_ref.at[:, cols], out_hbm.at[:, cols], out_sem.at[c]).wait()
+
     for target in order[:-1]:
         ready_copy(z, target).wait_send()
+        along_copy(z, target).wait_send()
+    for group in relayed:
+        for other in others:
+            plane_copy(group, other).wait_send()
+        for other in others + [chip]:
+            pair_copy(group, other).wait_send()
     for k in range(seqs):
         @pl.when(k > me)
         def _():
@@ -178,17 +256,15 @@
     feats = w_qkv.shape[2]
     heads = feats // DH
     seqs, groups = lax.axis_size("seq"), lax.axis_size("head")
-    share = w_out.shape[0] // seqs
-    mine = lax.dynamic_slice_in_dim(w_out, lax.axis_index("seq") * share, share, axis=0)
-    w_all = lax.all_gather(mine, ("head", "seq"), axis=0, tiled=True)
     piece = tokens // groups
-    regrouped = pl.pallas_call(
+    return pl.pallas_call(
         functools.partial(mix_kernel, seqs, groups),
-        out_shape=jax.ShapeDtypeStruct((piece, groups * feats), jnp.bfloat16),
+        out_shape=jax.ShapeDtypeStruct((piece, w_out.shape[1]), jnp.bfloat16),
         in_specs=[
             pl.BlockSpec(memory_space=pl.ANY),
             pl.BlockSpec(memory_space=pl.ANY),
             pl.BlockSpec(memory_space=pltpu.VMEM),
+            pl.BlockSpec(memory_space=pl.ANY),
         ],
         out_specs=pl.BlockSpec(memory_space=pl.ANY),
         scratch_shapes=[
@@ -202,6 +278,10 @@
             pltpu.VMEM((heads, DH, DH), jnp.bfloat16),
             pltpu.VMEM((seqs, heads, DH, DH), jnp.bfloat16),
             pltpu.VMEM((groups, piece, feats), jnp.bfloat16),
+            pltpu.VMEM((groups, piece, feats), jnp.bfloat16),
+            pltpu.VMEM((groups * feats, w_out.shape[1]), jnp.bfloat16),
+            pltpu.VMEM((piece, w_out.shape[1]), jnp.float32),
+            pltpu.VMEM((piece, w_out.shape[1]), jnp.bfloat16),
             pltpu.SemaphoreType.DMA((groups,)),
             pltpu.SemaphoreType.DMA((3,)),
             pltpu.SemaphoreType.DMA,
@@ -209,6 +289,11 @@
             pltpu.SemaphoreType.DMA((seqs,)),
             pltpu.SemaphoreType.DMA((groups,)),
             pltpu.SemaphoreType.DMA((groups,)),
+            pltpu.SemaphoreType.DMA((groups,)),
+            pltpu.SemaphoreType.DMA((groups, seqs // 2)),
+            pltpu.SemaphoreType.DMA((groups, seqs // 2)),
+            pltpu.SemaphoreType.DMA((groups, seqs)),
+            pltpu.SemaphoreType.DMA((w_out.shape[1] // feats,)),
         ],
         compiler_params=pltpu.CompilerParams(
             collective_id=0, has_side_effects=True, vmem_limit_bytes=56 * 2**20
@@ -218,8 +303,7 @@
             bytes_accessed=2 * (tokens * width + 3 * width * feats) + 200 * 10**6,
             transcendentals=0,
         ),
-    )(inputs, w_qkv, norm_gain.reshape(1, feats))
-    return jnp.dot(regrouped, w_all, preferred_element_type=jnp.float32).astype(jnp.bfloat16)
+    )(inputs, w_qkv, norm_gain.reshape(1, feats), w_out)
 
 
 def solution(mesh):

time: 138 us -> 84.6 us (0.61)
  waiting for transfers between devices: 49.9 us -> 0 us
  Pallas kernels: 62.5 us -> 80.3 us
  between operations: 13.4 us -> 0.01 us
  matrix products: 9.83 us -> 0 us
    all_gather x1 -> x0, waiting for transfers between devices: 49.8 us -> none  [on_device(): w_all = lax.all_gather(mine, ('head', 'seq'), axis=0, tiled=True)]
    pallas_call x1, Pallas kernels: 62.5 us -> 80.3 us  [on_device(): pl.pallas_call(functools.partial(mix_kernel, seqs, groups), out_shape=jax...]
    dot_general x1 -> x0, matrix products: 9.83 us -> none  [on_device(): jnp.dot(regrouped, w_all, preferred_element_type=jnp.float32)]
    unnamed x2 -> x1, local copies, waits for them, and re-layouts: 1.59 us -> 3.16 us
  transfers between devices with their start and end apart: 1 -> 0, of which waited for: 1 -> 0; matrix products, arithmetic and copies ran while one was open for 0% -> 0% of each run, Pallas kernels for 45% -> 0%
where the time goes in v3:
time: 84.6 us; the launch traced here: 83.5 us
  Pallas kernels  80.3 us (95%)
  local copies, waits for them, and re-layouts  3.16 us (4%)
    pallas_call x1, Pallas kernels, on_device(): pl.pallas_call(functools.partial(mix_kernel, seqs, groups), out_shape=jax...  80.3 us
    unnamed x1, local copies, waits for them, and re-layouts  3.16 us

profile of v3, /device:TPU:0, one launch (start us, length us, event | category | flops | bytes accessed | tf_op | source)
XLA Modules:
  0.0 83.5 jit_solution(13878842974903712988)
XLA Ops:
  0.0 80.3 %shard_map.46 = bf16[512,2048]{1,0:T(8,128)(2,1)} custom-call(bf16[2048,2048]{1,0:T(8,128)(2,1)} %x_hbm.1, bf16[3,2048,512]{2,1,0:T(8,128)(2,1)} %w_hbm.1, f32[1,512]{1,0:T(1,128)} %bitcast.1, bf16[512,2048]{1,0:T(8,128)(2,1)} %wo_hbm.1), custom_call_target="tpu_custom_call" | custom-call | flops 15032385536 | bytes 214680064 | tf_op jit(solution)/shard_map/pallas_call | solution.py:260
  80.3 3.2 %copy.6 = bf16[512,2048]{1,0:T(8,128)(2,1)} copy(bf16[512,2048]{1,0:T(8,128)(2,1)} %shard_map.46) | data formatting | bytes 4194304

commit v4 on v3

--- a/solution.py
+++ b/solution.py
@@ -53,12 +53,29 @@
     def own_share():
         return wo_hbm.at[pl.ds(pl.multiple_of(me * share, share), share)]
 
-    def along_copy(source, target):
+    def along_copy(mask, bit):
+        group = flipped(z, mask)
+        rows = wo_ref.at[wo_rows(group, me)]
         return pltpu.make_async_remote_copy(
-            src_ref=own_share(), dst_ref=wo_ref.at[wo_rows(source, me)],
-            send_sem=along_send.at[target], recv_sem=wo_recv.at[source, me],
-            device_id=(me, target), device_id_type=MESH,
-        )
+            src_ref=rows if mask else own_share(), dst_ref=rows,
+            send_sem=along_send.at[mask + bit], recv_sem=wo_recv.at[group, me],
+            device_id=(me, flipped(z, bit)), device_id_type=MESH,
+        )
+
+    def along_wait(mask):
+        relay_copy(flipped(z, mask), me, me, along_send.at[mask]).wait_recv()
+
+    def spread(mask):
+        group = flipped(z, mask)
+        for other in others:
+            plane_copy(group, other).start()
+        pair_copy(group, chip).start()
+
+    bits = [1 << b for b in reversed(range(groups.bit_length() - 1))]
+    hops = [
+        (mask, bit) for mask in range(groups) for bit in bits
+        if mask == 0 or bit < (mask & -mask)
+    ]
 
     def relay_copy(group, seq, target, send):
         return pltpu.make_async_remote_copy(
@@ -101,12 +118,10 @@
 
     total[...] = jnp.zeros_like(total)
     pl.semaphore_wait(barrier, seqs + groups - 2)
-    for target in order[:-1]:
-        along_copy(z, target).start()
+    for bit in bits:
+        along_copy(0, bit).start()
     own_wo.wait()
-    for other in others:
-        plane_copy(z, other).start()
-    pair_copy(z, chip).start()
+    spread(0)
     w_copy(1).wait()
 
     for c in range(groups):
@@ -146,6 +161,13 @@
         def _():
             state_copy(me, k).start()
 
+    relays = []
+    for mask, bit in hops:
+        if mask:
+            if mask not in relays:
+                along_wait(mask)
+                relays.append(mask)
+            along_copy(mask, bit).start()
     w_copy(0).wait()
     for c in range(groups):
         rows = pl.ds(c * piece, piece)
@@ -160,11 +182,13 @@
             state_copy(k, me).wait_recv()
             total[...] += arrived[k].astype(jnp.float32)
 
-    for group in order[:-1]:
-        along_copy(group, group).wait_recv()
-        for other in others:
-            plane_copy(group, other).start()
-        pair_copy(group, chip).start()
+    late = [mask for mask in range(1, groups) if mask not in relays and mask not in bits]
+    for mask in relays:
+        spread(mask)
+    for mask in bits:
+        if mask not in relays:
+            along_wait(mask)
+            spread(mask)
 
     lower = lax.broadcasted_iota(jnp.int32, (BLK, BLK), 0) >= lax.broadcasted_iota(
         jnp.int32, (BLK, BLK), 1
@@ -187,22 +211,26 @@
         mean_sq = jnp.mean(attended * attended, axis=-1, keepdims=True)
         return (attended * lax.rsqrt(mean_sq + EPS) * gain_ref[:, cols]).astype(jnp.bfloat16)
 
-    def ready_copy(source, target):
+    def ready_copy(source, target, b):
+        rows = pl.ds(b * BLK, BLK)
         return pltpu.make_async_remote_copy(
-            src_ref=ready.at[target],
-            dst_ref=landed.at[source],
-            send_sem=send_sem.at[target], recv_sem=recv_sem.at[source],
+            src_ref=ready.at[target, rows], dst_ref=landed.at[source, rows],
+            send_sem=send_sem.at[target, b], recv_sem=recv_sem.at[source, b],
             device_id=(me, target), device_id_type=MESH,
         )
 
-    for target in order:
+    for step, target in enumerate(order):
         for b in range(blocks):
             for h in range(heads):
                 ready[target, pl.ds(b * BLK, BLK), pl.ds(h * DH, DH)] = attend(
                     target * blocks + b, h
                 )
-        if target is not order[-1]:
-            ready_copy(z, target).start()
+            if step < groups - 1:
+                ready_copy(z, target, b).start()
+        if step == 0:
+            for mask in late:
+                along_wait(mask)
+                spread(mask)
 
     relayed = [z] + order[:-1]
     for group in relayed:
@@ -218,7 +246,8 @@
                 group, other * 2 + 1 - core, me, pair_send.at[group, other]
             ).wait_recv()
         if step > 0:
-            ready_copy(group, group).wait_recv()
+            for b in range(blocks):
+                ready_copy(group, group, b).wait_recv()
         source = ready if step == 0 else landed
         rows = pl.ds(pl.multiple_of(group * feats, feats), feats)
         for c in range(width // columns):
@@ -238,8 +267,10 @@
         pltpu.make_async_copy(out_ref.at[:, cols], out_hbm.at[:, cols], out_sem.at[c]).wait()
 
     for target in order[:-1]:
-        ready_copy(z, target).wait_send()
-        along_copy(z, target).wait_send()
+        for b in range(blocks):
+            ready_copy(z, target, b).wait_send()
+    for mask, bit in hops:
+        along_copy(mask, bit).wait_send()
     for group in relayed:
         for other in others:
             plane_copy(group, other).wait_send()
@@ -287,8 +318,8 @@
             pltpu.SemaphoreType.DMA,
             pltpu.SemaphoreType.DMA((seqs,)),
             pltpu.SemaphoreType.DMA((seqs,)),
-            pltpu.SemaphoreType.DMA((groups,)),
-            pltpu.SemaphoreType.DMA((groups,)),
+            pltpu.SemaphoreType.DMA((groups, piece // BLK)),
+            pltpu.SemaphoreType.DMA((groups, piece // BLK)),
             pltpu.SemaphoreType.DMA((groups,)),
             pltpu.SemaphoreType.DMA((groups, seqs // 2)),
             pltpu.SemaphoreType.DMA((groups, seqs // 2)),

time: 84.6 us -> 84 us (level)
  the two profiles are of different devices: /device:TPU:0 before, /device:TPU:10 now
where the time goes in v4:
time: 84 us; the launch traced here: 83.8 us
  Pallas kernels  80.6 us (96%)
  local copies, waits for them, and re-layouts  3.16 us (4%)
    pallas_call x1, Pallas kernels, on_device(): pl.pallas_call(functools.partial(mix_kernel, seqs, groups), out_shape=jax...  80.6 us
    unnamed x1, local copies, waits for them, and re-layouts  3.16 us

profile of v4, /device:TPU:10, one launch (start us, length us, event | category | flops | bytes accessed | tf_op | source)
XLA Modules:
  0.0 83.8 jit_solution(3469689335765877133)
XLA Ops:
  0.0 80.6 %shard_map.46 = bf16[512,2048]{1,0:T(8,128)(2,1)} custom-call(bf16[2048,2048]{1,0:T(8,128)(2,1)} %x_hbm.1, bf16[3,2048,512]{2,1,0:T(8,128)(2,1)} %w_hbm.1, f32[1,512]{1,0:T(1,128)} %bitcast.1, bf16[512,2048]{1,0:T(8,128)(2,1)} %wo_hbm.1), custom_call_target="tpu_custom_call" | custom-call | flops 15032385536 | bytes 214680064 | tf_op jit(solution)/shard_map/pallas_call | solution.py:291
  80.6 3.2 %copy.6 = bf16[512,2048]{1,0:T(8,128)(2,1)} copy(bf16[512,2048]{1,0:T(8,128)(2,1)} %shard_map.46) | data formatting | bytes 4194304
